TPU v7x, 128 devices: a whole 4x4x4 slice. The times are simulated.
128 devices in a mesh: state: 16 (over y, x_hi, core), walk: 8 (over z, x_lo).
Axes of the slice: x: 4 (x_hi: 2, x_lo: 2; x = x_hi * 2 + x_lo), y: 4, z: 4, core: 2. Of those that a mesh axis runs over, the one named last changes fastest.
Arguments:
- features: bfloat16 [16, 8, 512, 256], P('state', 'walk'), may hold values from -6 to 6
- key_blocks: int32 [16, 8, 4, 3], P('state', 'walk'), may hold values from 0 to 3, as said below
- block_counts: int32 [16, 8, 4], P('state', 'walk'), may hold values from 1 to 3, as said below
- potential: float32 [16, 8], P('state', 'walk'), may hold values from -14 to -0.7
- w_qkv: bfloat16 [16, 2, 256, 768], P('state'), may hold values from -1 to 1
- w_out: bfloat16 [16, 2, 256, 256], P('state'), may hold values from -0.375 to 0.375
- w_up: bfloat16 [16, 2, 256, 512], P('state'), may hold values from -0.375 to 0.375
- w_down: bfloat16 [16, 2, 512, 256], P('state'), may hold values from -0.25 to 0.25
- gains: float32 [16, 5, 256], P('state'), may hold values from 0.25 to 1.75
- readouts: float32 [16, 2, 256], P('state'), may hold values from -0.375 to 0.375
Outputs:
- energies: float32 [16, 16, 8], P('state', None, 'walk')
- mean_energy: float32 [16, 16], P('state')
Inputs may be any that keep to these rules, and one draw needn't show every extreme that they name: `key_blocks`: slot 0 of block b's list is b itself; the entries of a list are distinct blocks; entries at slots at or past the count are ignored. `block_counts`: block 0 of every configuration has a full list of 3 blocks.
All inputs are finite; a program needn't handle non-finite values.
Results may differ from a plain program's by a relative error of at most 0.04.
Values may be sent and summed in bfloat16 or wider, within the bound.
A program may use at most 128 MiB of HBM per device.

v0:
```python
import jax
import jax.numpy as jnp
from jax import lax
from jax.sharding import PartitionSpec as P

HEADS = 8
BLOCK = 128


def rms_norm(value, gain):
    return value * lax.rsqrt(jnp.mean(value * value, axis=-1, keepdims=True) + 1e-06) * gain


def evaluate(w_qkv, w_out, w_up, w_down, gains, readouts, feats, lists, counts):
    atoms, width = feats.shape
    nblocks = atoms // BLOCK
    slots = lists.shape[-1]
    head_dim = width // HEADS
    hidden = feats.astype(jnp.float32)
    valid = jnp.arange(slots)[None, :] < counts[:, None]
    keymask = jnp.repeat(valid, BLOCK, axis=1)
    layers = w_qkv.shape[0]
    for layer in range(layers):
        normed = rms_norm(hidden, gains[2 * layer]).astype(jnp.bfloat16)
        proj = jnp.dot(normed, w_qkv[layer], preferred_element_type=jnp.float32).astype(
            jnp.bfloat16
        )
        query = proj[:, :width].reshape(nblocks, BLOCK, HEADS, head_dim)
        keyval = proj[:, width:].reshape(nblocks, BLOCK, 2 * width)
        picked = keyval[lists].reshape(nblocks, slots * BLOCK, 2 * width)
        keys = picked[:, :, :width].reshape(nblocks, slots * BLOCK, HEADS, head_dim)
        values = picked[:, :, width:].reshape(nblocks, slots * BLOCK, HEADS, head_dim)
        scores = jnp.einsum(
            "qahd,qkhd->qhak", query, keys, preferred_element_type=jnp.float32
        ) / jnp.sqrt(jnp.float32(head_dim))
        scores = jnp.where(keymask[:, None, None, :], scores, jnp.float32(-1e30))
        top = jnp.max(scores, axis=-1, keepdims=True)
        expo = jnp.exp(scores - top)
        probs = (expo / jnp.sum(expo, axis=-1, keepdims=True)).astype(jnp.bfloat16)
        attended = jnp.einsum("qhak,qkhd->qahd", probs, values, preferred_element_type=jnp.float32)
        attended = attended.astype(jnp.bfloat16).reshape(atoms, width)
        hidden = hidden + jnp.dot(attended, w_out[layer], preferred_element_type=jnp.float32)
        normed = rms_norm(hidden, gains[2 * layer + 1]).astype(jnp.bfloat16)
        upper = jax.nn.gelu(
            jnp.dot(normed, w_up[layer], preferred_element_type=jnp.float32)
        ).astype(jnp.bfloat16)
        hidden = hidden + jnp.dot(upper, w_down[layer], preferred_element_type=jnp.float32)
    final = rms_norm(hidden, gains[2 * layers])
    pooled = jnp.sum(final, axis=0) / jnp.sqrt(jnp.float32(atoms))
    return (jnp.sum(pooled * readouts[0]), jnp.sum(pooled * readouts[1]))


def solve_batched(matrix, right):
    size = matrix.shape[0]

    def step(k, state):
        mat, rhs = state
        pivot_row = lax.dynamic_index_in_dim(mat, k, 0, keepdims=False)
        pivot = lax.dynamic_index_in_dim(pivot_row, k, 0, keepdims=False)
        scaled = pivot_row / pivot[None, :]
        scaled_rhs = lax.dynamic_index_in_dim(rhs, k, 0, keepdims=False) / pivot[None, :]
        column = lax.dynamic_index_in_dim(mat, k, 1, keepdims=False)
        is_row = (jnp.arange(size) == k)[:, None, None]
        mat = jnp.where(is_row, scaled[None], mat - column[:, None, :] * scaled[None])
        rhs = jnp.where(is_row, scaled_rhs[None], rhs - column[:, None, :] * scaled_rhs[None])
        return (mat, rhs)

    return lax.fori_loop(0, size, step, (matrix, right))[1]


def local(
    features, key_blocks, block_counts, potential, w_qkv, w_out, w_up, w_down, gains, readouts
):
    states = lax.axis_size("state")
    index = lax.axis_index("state")
    walkers = features.shape[1]
    atoms, width = (features.shape[2], features.shape[3])
    nblocks, slots = (key_blocks.shape[2], key_blocks.shape[3])
    onehot = (jnp.arange(states) == index).astype(jnp.float32)[:, None]
    feats = lax.all_gather(features, "state", axis=0, tiled=True)
    lists = lax.all_gather(key_blocks, "state", axis=0, tiled=True)
    counts = lax.all_gather(block_counts, "state", axis=0, tiled=True)
    count = feats.shape[0]

    def one_config(args):
        return evaluate(
            w_qkv[0], w_out[0], w_up[0], w_down[0], gains[0], readouts[0], args[0], args[1], args[2]
        )

    amp, ham = lax.map(
        one_config,
        (
            feats.reshape(count * walkers, atoms, width),
            lists.reshape(count * walkers, nblocks, slots),
            counts.reshape(count * walkers, nblocks),
        ),
    )
    amp_row = amp.reshape(count, walkers)
    ham_row = ham.reshape(count, walkers)
    psi_row = onehot + 0.9 / states * jnp.tanh(amp_row)
    psi, ham = (
        lax.all_gather(psi_row[None], "state", axis=0, tiled=True),
        lax.all_gather(ham_row[None], "state", axis=0, tiled=True),
    )
    solution = solve_batched(psi, ham)
    energy_rows = lax.dynamic_index_in_dim(solution, index, 0, keepdims=True)
    energy_rows = energy_rows + onehot[None] * potential[:, None, :]
    totals = lax.psum(jnp.sum(energy_rows, axis=-1), "walk")
    mean_energy = totals / (walkers * lax.axis_size("walk"))
    return (energy_rows, mean_energy)


def solution(mesh):
    placed = (
        P("state", "walk", None, None),
        P("state", "walk", None, None),
        P("state", "walk", None),
        P("state", "walk"),
        P("state", None, None, None),
        P("state", None, None, None),
        P("state", None, None, None),
        P("state", None, None, None),
        P("state", None, None),
        P("state", None, None),
    )
    return jax.shard_map(
        local,
        mesh=mesh,
        in_specs=placed,
        out_specs=(P("state", None, "walk"), P("state", None)),
        check_vma=False,
    )
```

profile of v0, /device:TPU:0, one launch (start us, length us, event | category | flops | bytes accessed | tf_op | source)
XLA Modules:
  0.0 744.9 jit_solution(8173098407457888753)
XLA Ops:
  7.9 24.9 %all_gather.16 = s32[16,1,4,3]{2,1,3,0:T(1,128)S(1)} all-gather(s32[1,1,4,3]{2,1,3,0:T(1,128)} %param.15), channel_id=1, replica_groups=mesh['state'=16,'walk'=8] {'state'}, dimensions={0}, use_global_device_ids=true | all-gather | bytes 816 | tf_op jit(solution)/shard_map/all_gather | solution.py:81
  35.6 19.3 %all_gather.17 = s32[16,1,4]{2,1,0:T(1,128)S(1)} all-gather(s32[1,1,4]{2,1,0:T(1,128)} %param.16), channel_id=1, replica_groups=mesh['state'=16,'walk'=8] {'state'}, dimensions={0}, use_global_device_ids=true | all-gather | bytes 272 | tf_op jit(solution)/shard_map/all_gather | solution.py:82
  54.9 13.2 %all-gather.4.cloned.1.call-done = bf16[16,1,512,256]{3,2,1,0:T(8,128)(2,1)} async-done(((bf16[1,1,512,256]{3,2,1,0:T(8,128)(2,1)}), bf16[16,1,512,256]{3,2,1,0:T(8,128)(2,1)}) %all-gather.4.cloned.1.call-update) | async-done | bytes 4194320 | tf_op jit(solution)/shard_map/all_gather | solution.py:80
  68.2 587.5 %while.27 = (s32[]{:T(128)}, f32[16]{0:T(128)S(1)}, f32[16]{0:T(128)S(1)}, bf16[16,512,256]{2,1,0:T(8,128)(2,1)}, f32[1,5,256]{2,0,1:T(1,128)}, /*index=5*/bf16[...) while((s32[]{:T(128)}, f32[16]{0:T(128)S(1)}, ...), condition=%wide.region_13.14_spmd, body=%wide.region_0.13_spmd.sunk | while | flops 1505236224 | bytes 85344672 | solution.py:90
  90.7 5.9 fusion.186
  127.4 5.9 fusion.186
  164.1 5.9 fusion.186
  200.9 5.9 fusion.186
  237.6 5.9 fusion.186
  258.8 4.7 fusion.183
  274.3 5.9 fusion.186
  311.0 5.9 fusion.186
  347.7 5.9 fusion.186
  384.5 5.9 fusion.186
  421.2 5.9 fusion.186
  457.9 5.9 fusion.186
  494.6 5.9 fusion.186
  531.3 5.9 fusion.186
  568.1 5.9 fusion.186
  604.8 5.9 fusion.186
  641.5 5.9 fusion.186
  656.0 34.1 %all-reduce.2 = (f32[256]{0:T(256)S(1)}, f32[256]{0:T(256)S(1)}) all-reduce(f32[256]{0:T(256)S(1)} %fusion.118, f32[256]{0:T(256)S(1)} %dynamic-update-slice.1), channel_id=2, replica_groups=mesh['state'=16,'walk'=8] {'state'}, use_global_device_ids=true, to_apply=%add | all-reduce | flops 512 | bytes 4096
  690.3 26.8 %while.28 = (s32[]{:T(128)}, f32[16,16,1]{1,2,0:T(1,128)S(1)}, f32[16,16,1]{1,2,0:T(1,128)S(1)}, s32[]{:T(128)}, s32[]{:T(128)}, /*index=5*/s32[]{:T(128)}) while((s32[]{:T(128)}, f32[16,16,1]{1,2,0:T(1,128)S(1)}, f32[16,16,1]{1,2,0:T(1,128)S(1)}, s32[]{:T(128)}, s32[]{:T(128)}, /*index=5*/s32[]{:T(128)}) %tuple.94), condition=%wide.region_15.16_spmd, body=%wide.region_14.15_spmd.sunk | while | flops 1587 | bytes 4817 | solution.py:68
  717.1 19.9 %psum.7 = f32[1,16]{1,0:T(1,128)S(1)} all-reduce(f32[1,16]{1,0:T(1,128)S(1)} %fusion.144), channel_id=1, replica_groups=mesh['state'=16,'walk'=8] {'walk'}, use_global_device_ids=true, to_apply=%region_16.17 | all-reduce | flops 16 | bytes 128 | tf_op jit(solution)/shard_map/psum | solution.py:108
  (1151 shorter events, 513.7 us)
Async XLA Ops:
  7.2 61.0 %all-gather.4.cloned.1.call-start = ((), (), s32[]{:S(2)}) async-start(), calls=%async_computation | async-start | bytes 4456448 | tf_op jit(solution)/shard_map/all_gather | solution.py:80
  80.3 6.6 copy-start.5
  90.4 6.1 copy-start
  117.0 6.6 copy-start.5
  153.7 6.6 copy-start.5
  190.4 6.6 copy-start.5
  200.6 6.1 copy-start
  227.1 6.6 copy-start.5
  237.3 6.1 copy-start
  263.9 6.6 copy-start.5
  300.6 6.6 copy-start.5
  310.8 6.1 copy-start
  337.3 6.6 copy-start.5
  374.0 6.6 copy-start.5
  410.7 6.6 copy-start.5
  420.9 6.1 copy-start
  447.5 6.6 copy-start.5
  484.2 6.6 copy-start.5
  520.9 6.6 copy-start.5
  531.1 6.1 copy-start
  557.6 6.6 copy-start.5
  594.4 6.6 copy-start.5
  631.1 6.6 copy-start.5
  641.3 6.1 copy-start
  (121 other events, 401.3 us)
Sparse Core Ops, SparseCore 0:
  10.5 57.6 all-gather.3
where the time goes:
time: 748 us; the launch traced here: 745 us
  matrix products  387 us (52%)
  local copies, waits for them, and re-layouts  195 us (26%)
  blocking collectives  98.2 us (13%)
  other arithmetic  29.4 us (4%)
  between operations  15.4 us (2%)
  waiting for transfers between devices  13.9 us (2%)
    sub x32, matrix products, evaluate(): expo = jnp.exp(scores - top)  169 us
    dot_general x32, matrix products, evaluate(): jnp.einsum('qhak,qkhd->qahd', probs, values, preferred_element_type=jnp.f...  133 us
    while x352, local copies, waits for them, and re-layouts  53.7 us
    dot_general x32, matrix products, evaluate(): jnp.dot(upper, w_down[layer], preferred_element_type=jnp.float32)  44.1 us
    unnamed x1, blocking collectives  34.1 us
    dot_general x32, matrix products, evaluate(): jnp.dot(normed, w_qkv[layer], preferred_element_type=jnp.float32)  31.5 us
    all_gather x1, blocking collectives, local(): lists = lax.all_gather(key_blocks, 'state', axis=0, tiled=True)  24.9 us
    dynamic_update_slice x32, local copies, waits for them, and re-layouts, local(): lax.map(one_config, (feats.reshape(count * walkers, atoms, width), lists....  23 us
  transfers between devices with their start and end apart: 1, of which 1 were waited for; matrix products, arithmetic and copies ran while one was open for 0% of the time, Pallas kernels for 0%

commit v1 on v0

v1 whole, which is shorter than its diff:
```python
import functools

import jax
import jax.numpy as jnp
from jax import lax
from jax.experimental import pallas as pl
from jax.experimental.pallas import tpu as pltpu
from jax.sharding import PartitionSpec as P

D = 256
A = 512
B = 128
NB = 4
H = 8
SLOTS = 3
EXTRA = 16
EARLY = 4
QS = 1.4426950408889634 / 32.0**0.5
bf = jnp.bfloat16
f32 = jnp.float32
MESH = pl.DeviceIdType.MESH
V = pl.BlockSpec(memory_space=pltpu.VMEM)
ANY = pl.BlockSpec(memory_space=pl.ANY)


def mm(a, b):
    return lax.dot_general(a, b, (((1,), (0,)), ((), ())), preferred_element_type=f32)


def rscale(h):
    return lax.rsqrt(jnp.sum(h * h, axis=0, keepdims=True) * (1.0 / D) + 1e-6)


def norm(h, g):
    r = rscale(h)
    parts = [((h[:, c : c + 128] * r[:, c : c + 128]) * g).astype(bf) for c in range(0, h.shape[1], 128)]
    return jnp.concatenate(parts, axis=1)


class Net:
    def __init__(self, weights, scratch):
        self.wqkv, self.wo, self.wu, self.wd, self.gn, self.gr = weights
        self.h, self.k, self.v, self.qx, self.a, self.lim, self.ivm, self.ism, self.isem, self.xbuf, self.xsem = scratch

    def clear(self):
        self.qx[...] = jnp.zeros(self.qx.shape, bf)
        self.v[...] = jnp.ones(self.v.shape, bf)
        self.lim[...] = jnp.ones(self.lim.shape, f32)

    def ints(self, s):
        self.ivm[...] = self.xbuf[s, D : D + EXTRA, 0:128].astype(f32).astype(jnp.int32)
        return pltpu.make_async_copy(self.ivm, self.ism.at[s], self.isem)

    def project(self, l, c, h):
        n = norm(h, self.gn[2 * l])
        q = (mm(self.wqkv[l, 0:256, :], n) * QS).astype(bf)
        k = mm(self.wqkv[l, 256:512, :], n).astype(bf).T
        v = mm(self.wqkv[l, 512:768, :], n).astype(bf)
        for head in range(H):
            row, lane = (head % 4) * 32, (head % 2) * 128
            for b in range(2):
                self.qx[2 * c + b, head // 2, row : row + 32, lane : lane + 128] = q[
                    head * 32 : head * 32 + 32, b * 128 : b * 128 + 128
                ]
        for b in range(2):
            self.k[2 * c + b] = k[b * 128 : b * 128 + 128, :]
            for p in range(4):
                self.v[2 * c + b, p, 0:64, :] = v[p * 64 : p * 64 + 64, b * 128 : b * 128 + 128]

    def scores(self, b, kbs, p):
        half = p // 2 * 128
        return [mm(self.k[kb, :, half : half + 128], self.qx[b, p]) for kb in kbs]

    def mix(self, ss, kbs, p, keep, safe):
        if safe:
            top = functools.reduce(jnp.maximum, [jnp.max(s, axis=0, keepdims=True) for s in ss])
            ss = [s - top for s in ss]
        ps = [jnp.exp2(s).astype(bf) for s in ss]
        if keep is not None:
            ps = [jnp.where(ok, q, jnp.zeros_like(q)) if s else q for s, (ok, q) in enumerate(zip(keep, ps))]
        vs = [self.v[kb, p] for kb in kbs]
        return mm(jnp.concatenate(vs, axis=1), jnp.concatenate(ps, axis=0))

    def emit(self, o, b, p):
        den = o[64:72, :]
        inv = 1.0 / den[0:1]
        lanes = pl.ds(pl.multiple_of(b * 128, 128), 128)
        self.a[p * 64 : p * 64 + 32, lanes] = (o[0:32, :128] * inv[:, :128]).astype(bf)
        self.a[p * 64 + 32 : p * 64 + 64, lanes] = (o[32:64, 128:] * inv[:, 128:]).astype(bf)
        return den

    def attend(self, items, safe):
        units = [(b, kbs, keep, p) for p in range(4) for b, kbs, keep in items]
        ss = [self.scores(b, kbs, p) for b, kbs, _, p in units]
        outs = [self.mix(s, kbs, p, keep, safe) for s, (_, kbs, keep, p) in zip(ss, units)]
        dens = [self.emit(o, b, p) for o, (b, _, _, p) in zip(outs, units)]
        if not safe:
            self.lim[0] = jnp.minimum(self.lim[0], functools.reduce(jnp.minimum, dens))
            self.lim[1] = jnp.maximum(self.lim[1], functools.reduce(jnp.maximum, dens))

    def attention_masked(self, s):
        def two(g, _):
            items = []
            for b in (2 * g, 2 * g + 1):
                count = self.ism[s, 0, SLOTS * NB + b]
                kbs = [jnp.clip(self.ism[s, 0, b * SLOTS + t], 0, NB - 1) for t in range(SLOTS)]
                items.append((b, kbs, [count > t for t in range(SLOTS)]))
            self.attend(items, False)
            return 0

        lax.fori_loop(0, NB // 2, two, 0)

    def attention(self, s, safe):
        def two(g, _):
            x, y = self.ism[s, 0, SLOTS * NB + 2 * g], self.ism[s, 0, SLOTS * NB + 2 * g + 1]
            swap = (y > x).astype(jnp.int32)
            more, less = 2 * g + swap, 2 * g + 1 - swap
            most, least = jnp.maximum(x, y), jnp.minimum(x, y)

            def run(c0, c1):
                lists = [(b, [self.ism[s, 0, b * SLOTS + t] for t in range(c)], None) for b, c in ((more, c0), (less, c1))]
                self.attend(lists, safe)

            for c0 in range(1, SLOTS + 1):
                for c1 in range(1, c0 + 1):
                    pl.when((most == c0) & (least == c1))(functools.partial(run, c0, c1))
            return 0

        lax.fori_loop(0, NB // 2, two, 0)

    def feed(self, l, then):
        cols = [slice(c * 256, c * 256 + 256) for c in range(2)]
        hs = [self.h[:, s] + mm(self.wo[l], self.a[:, s]) for s in cols]
        us = [mm(self.wu[l], norm(h, self.gn[2 * l + 1])) for h in hs]
        for c in range(2):
            u = us[c]
            z = u * (0.7978845608028654 + 0.035677408136300125 * (u * u))
            half = 0.5 * u
            g = (half + half * jnp.tanh(z)).astype(bf)
            then(c, hs[c] + mm(self.wd[l], g))

    def final(self, h, sums):
        r = rscale(h)
        out = []
        for t in range(2):
            g, acc = self.gr[t], sums[t]
            for c in range(0, h.shape[1], 128):
                acc = acc + jnp.sum(h[:, c : c + 128] * g, axis=0, keepdims=True) * r[:, c : c + 128]
            out.append(acc)
        return out

    def run(self, first, count, attention, fetch, out, at, between=None):
        def begin(s):
            return [self.xbuf[s, 0:D, c * 256 : c * 256 + 256].astype(f32) for c in range(2)]

        s0 = first % 2
        fetch(first).start()
        fetch(first).wait()
        lists = self.ints(s0)
        lists.start()
        for c, h in enumerate(begin(s0)):
            self.h[:, c * 256 : c * 256 + 256] = h
            self.project(0, c, h)
        lists.wait()

        def config(i, _):
            s = lax.rem(i, 2)
            if between is not None:
                between(i)

            @pl.when(i + 1 < first + count)
            def _():
                fetch(i + 1).start()

            def layer(l, _):
                attention(s)

                @pl.when(l == 0)
                def _():
                    def then(c, h):
                        self.h[:, c * 256 : c * 256 + 256] = h
                        self.project(1, c, h)

                    self.feed(0, then)

                @pl.when(l == 1)
                def _():
                    @pl.when(i + 1 < first + count)
                    def _():
                        fetch(i + 1).wait()
                        lists = self.ints(1 - s)
                        lists.start()
                        lists.wait()

                    sums = [[0.0, 0.0]]
                    later = begin(1 - s)
                    for c in range(2):
                        self.project(0, c, later[c])
                    self.feed(1, lambda c, h: sums.append(self.final(h, sums[-1])))
                    for c in range(2):
                        self.h[:, c * 256 : c * 256 + 256] = later[c]
                    for t in range(2):
                        out[t, pl.ds(i - at, 1)] = sums[-1][t]

                return 0

            lax.fori_loop(0, 2, layer, 0)
            return 0

        lax.fori_loop(first, first + count, config, 0)


def scratch():
    return [
        pltpu.VMEM((D, A), f32),
        pltpu.VMEM((NB, B, D), bf),
        pltpu.VMEM((NB, 4, 80, B), bf),
        pltpu.VMEM((NB, 4, B, 2 * B), bf),
        pltpu.VMEM((D, A), bf),
        pltpu.VMEM((2, 8, 2 * B), f32),
        pltpu.VMEM((EXTRA, 128), jnp.int32),
        pltpu.SMEM((2, EXTRA, 128), jnp.int32),
        pltpu.SemaphoreType.DMA,
        pltpu.VMEM((2, D + EXTRA, A), bf),
        pltpu.SemaphoreType.DMA((2,)),
    ]


def flip(me, k):
    out = 0
    for bit in (1, 2, 4, 8):
        mine = lax.rem(lax.div(me, bit), 2)
        out = out + bit * ((1 - mine) if k & bit else mine)
    return out


def gather_kernel(states, x_ref, *refs):
    weights, (all_ref, out, lims) = refs[:6], refs[6:9]
    net = Net(weights, refs[9:20])
    ssem, rsem, csem = refs[20:]
    me, mw = lax.axis_index("state"), lax.axis_index("walk")
    barrier = pltpu.get_barrier_semaphore()
    partners = [1] + list(range(2, states, 2))
    for k in partners:
        pl.semaphore_signal(barrier, inc=1, device_id=(flip(me, k), mw), device_id_type=MESH)
    own = pltpu.make_async_copy(x_ref, all_ref.at[0], csem)
    own.start()
    net.clear()
    pl.semaphore_wait(barrier, len(partners))

    def send(k):
        return pltpu.make_async_remote_copy(
            src_ref=x_ref, dst_ref=all_ref.at[k], send_sem=ssem.at[k], recv_sem=rsem.at[k],
            device_id=(flip(me, k), mw), device_id_type=MESH,
        )

    def relay(k):
        return pltpu.make_async_remote_copy(
            src_ref=all_ref.at[k], dst_ref=all_ref.at[k + 1], send_sem=ssem.at[k + 1], recv_sem=rsem.at[k + 1],
            device_id=(flip(me, 1), mw), device_id_type=MESH,
        )

    order = [1] + [k for k in ORDER if k < states]
    for k in order:
        send(k).start()
    own.wait()

    def fetch(i):
        s = lax.rem(i, 2)
        return pltpu.make_async_copy(all_ref.at[i], net.xbuf.at[s], net.xsem.at[s])

    def between(i):
        for n in range(EARLY):
            @pl.when(i == n)
            def _():
                if n + 1 < EARLY:
                    if n == 0:
                        send(1).wait_recv()
                    if n == 1:
                        send(2).wait_recv()
                        relay(2).start()
                    if n == 2:
                        relay(2).wait_recv()
                for k in BEFORE[n]:
                    send(k).wait_recv()
                    relay(k).start()

    net.run(0, EARLY, net.attention_masked, fetch, out, 0, between)
    done = {2} | {k for ks in BEFORE for k in ks}
    for k in order[1:]:
        if k not in done:
            send(k).wait_recv()
            relay(k).start()
    for k in order[1:]:
        if k != 2:
            relay(k).wait_recv()
    for k in order:
        send(k).wait_send()
    for k in order[1:]:
        relay(k).wait_send()
    lims[...] = net.lim[...]


ORDER = (2, 4, 12, 6, 14, 8, 10)
BEFORE = ((), (), (4, 12), (6, 14))


def gather(x, ws, states):
    return pl.pallas_call(
        functools.partial(gather_kernel, states),
        out_shape=(
            jax.ShapeDtypeStruct((states, D + EXTRA, A), bf),
            jax.ShapeDtypeStruct((2, EARLY, 128), f32),
            jax.ShapeDtypeStruct((2, 8, 2 * B), f32),
        ),
        in_specs=[ANY] + [V] * 6,
        out_specs=(ANY, V, V),
        scratch_shapes=scratch()
        + [pltpu.SemaphoreType.DMA((states,)), pltpu.SemaphoreType.DMA((states,)), pltpu.SemaphoreType.DMA],
        compiler_params=pltpu.CompilerParams(collective_id=1, has_side_effects=True, vmem_limit_bytes=56 * 2**20),
    )(x, *ws)


def rest_kernel(states, all_ref, early, lims, *refs):
    weights, out = refs[:6], refs[6]
    net = Net(weights, refs[7:])
    net.clear()

    def fetch(i):
        s = lax.rem(i, 2)
        return pltpu.make_async_copy(all_ref.at[i], net.xbuf.at[s], net.xsem.at[s])

    def within(lim):
        return (jnp.min(lim[0]) > 2.0**-80) & (jnp.max(lim[1]) < 2.0**100)

    out[:, 0:EARLY] = early[...]
    net.run(EARLY, states - EARLY, lambda s: net.attention(s, False), fetch, out, 0)

    @pl.when(jnp.logical_not(within(lims) & within(net.lim)))
    def _():
        net.run(0, states, lambda s: net.attention(s, True), fetch, out, 0)


def rest(every, early, lims, ws, states):
    return pl.pallas_call(
        functools.partial(rest_kernel, states),
        out_shape=jax.ShapeDtypeStruct((2, states, 128), f32),
        in_specs=[ANY] + [V] * 8,
        out_specs=V,
        scratch_shapes=scratch(),
        compiler_params=pltpu.CompilerParams(vmem_limit_bytes=56 * 2**20),
    )(every, early, lims, *ws)


def solve_kernel(states, walks, *refs):
    parts, pot, energy, mean, mat, rows, ssem, rsem, wssem, wrsem = refs
    me, mw = lax.axis_index("state"), lax.axis_index("walk")
    barrier = pltpu.get_barrier_semaphore()
    for d in range(1, states):
        pl.semaphore_signal(barrier, inc=1, device_id=(lax.rem(me + d, states), mw), device_id_type=MESH)
    for d in range(1, walks):
        pl.semaphore_signal(barrier, inc=1, device_id=(me, lax.rem(mw + d, walks)), device_id_type=MESH)

    lane = lax.broadcasted_iota(jnp.int32, (states, 128), 1)
    row_at = lax.broadcasted_iota(jnp.int32, (states, 128), 0)
    config = jnp.bitwise_xor(row_at, me)

    def spread(t):
        value = jnp.sum(parts[t], axis=1, keepdims=True)
        return jnp.sum(jnp.where(lane == config + (1 - t) * states, value, 0.0), axis=0, keepdims=True)

    lane1 = lane[0:1]
    amp = spread(0)
    ham = spread(1)
    eye = jnp.where(lane1 == me + states, 1.0, 0.0)
    psi = jnp.where(lane1 < states, 0.0, eye + 0.9 / states * jnp.tanh(amp))
    mat[pl.ds(me, 1), :] = ham + jnp.where(lane1 < 2 * states, psi, 0.0)
    pl.semaphore_wait(barrier, states - 1 + walks - 1)

    def send(d):
        return pltpu.make_async_remote_copy(
            src_ref=mat.at[pl.ds(me, 1)], dst_ref=mat.at[pl.ds(me, 1)], send_sem=ssem.at[d], recv_sem=rsem.at[d],
            device_id=(lax.rem(me + d, states), mw), device_id_type=MESH,
        )

    for d in range(1, states):
        send(d).start()
    for d in range(1, states):
        came = lax.rem(me + states - d, states)
        pltpu.make_async_remote_copy(
            src_ref=mat.at[pl.ds(me, 1)], dst_ref=mat.at[pl.ds(came, 1)], send_sem=ssem.at[d], recv_sem=rsem.at[d],
            device_id=(lax.rem(me + d, states), mw), device_id_type=MESH,
        ).wait_recv()
    m = mat[...]
    for k in range(states):
        pivot_row = m[k : k + 1, :]
        scaled = pivot_row / pivot_row[:, states + k : states + k + 1]
        column = m[:, states + k : states + k + 1]
        m = jnp.where(row_at == k, scaled, m - column * scaled)
    mine = jnp.sum(jnp.where(row_at == me, m, 0.0), axis=0, keepdims=True)
    mine = jnp.where(lane1 == me, mine + pot[...], mine)
    energy[...] = mine[:, :states]
    rows[pl.ds(mw, 1), :] = mine

    def send_row(d):
        return pltpu.make_async_remote_copy(
            src_ref=rows.at[pl.ds(mw, 1)], dst_ref=rows.at[pl.ds(mw, 1)], send_sem=wssem.at[d], recv_sem=wrsem.at[d],
            device_id=(me, lax.rem(mw + d, walks)), device_id_type=MESH,
        )

    for d in range(1, walks):
        send_row(d).start()
    for d in range(1, walks):
        came = lax.rem(mw + walks - d, walks)
        pltpu.make_async_remote_copy(
            src_ref=rows.at[pl.ds(mw, 1)], dst_ref=rows.at[pl.ds(came, 1)], send_sem=wssem.at[d], recv_sem=wrsem.at[d],
            device_id=(me, lax.rem(mw + d, walks)), device_id_type=MESH,
        ).wait_recv()
    mean[...] = (jnp.sum(rows[...], axis=0, keepdims=True) * (1.0 / walks))[:, :states]
    for d in range(1, states):
        send(d).wait_send()
    for d in range(1, walks):
        send_row(d).wait_send()


def solve(parts, potential, states, walks):
    dma = pltpu.SemaphoreType.DMA
    return pl.pallas_call(
        functools.partial(solve_kernel, states, walks),
        out_shape=(jax.ShapeDtypeStruct((1, states), f32), jax.ShapeDtypeStruct((1, states), f32)),
        in_specs=[V, V],
        out_specs=(V, V),
        scratch_shapes=[
            pltpu.VMEM((states, 128), f32),
            pltpu.VMEM((walks, 128), f32),
            dma((states,)), dma((states,)), dma((walks,)), dma((walks,)),
        ],
        compiler_params=pltpu.CompilerParams(collective_id=0, has_side_effects=True),
    )(parts, potential)


def local(features, key_blocks, block_counts, potential, w_qkv, w_out, w_up, w_down, gains, readouts):
    states, walks = lax.axis_size("state"), lax.axis_size("walk")
    ints = jnp.concatenate([key_blocks.reshape(-1), block_counts.reshape(-1)]).astype(bf)
    extra = jnp.pad(ints[None], ((0, EXTRA - 1), (0, A - ints.shape[0])))
    mine = jnp.concatenate([features[0, 0].T, extra], axis=0)
    g = gains[0]
    ws = (
        w_qkv[0].swapaxes(1, 2),
        w_out[0].swapaxes(1, 2),
        w_up[0].swapaxes(1, 2),
        w_down[0].swapaxes(1, 2),
        jnp.broadcast_to(g[0:4, :, None], (4, D, 128)),
        jnp.broadcast_to((g[4] * readouts[0] / jnp.sqrt(f32(A)))[:, :, None], (2, D, 128)),
    )
    every, early, lims = gather(mine, ws, states)
    parts = rest(every, early, lims, ws, states)
    energy, mean = solve(parts, potential, states, walks)
    return energy[:, :, None], mean


def solution(mesh):
    placed = (
        P("state", "walk", None, None),
        P("state", "walk", None, None),
        P("state", "walk", None),
        P("state", "walk"),
        P("state", None, None, None),
        P("state", None, None, None),
        P("state", None, None, None),
        P("state", None, None, None),
        P("state", None, None),
        P("state", None, None),
    )
    return jax.shard_map(
        local,
        mesh=mesh,
        in_specs=placed,
        out_specs=(P("state", None, "walk"), P("state", None)),
        check_vma=False,
    )
```

time: 748 us -> 275 us (0.37)
  matrix products: 387 us -> 0 us
  Pallas kernels: 0 us -> 259 us
  local copies, waits for them, and re-layouts: 195 us -> 13.2 us
  blocking collectives: 98.2 us -> 0 us
  other arithmetic: 29.4 us -> 1.5 us
  between operations: 15.4 us -> 1.37 us
  waiting for transfers between devices: 13.9 us -> 0 us
    pallas_call x0 -> x3, Pallas kernels: none -> 259 us  [the longest x1 193 us: rest(): pl.pallas_call(functools.partial(rest_kernel, states), out_shape=jax.Shap...]
    dot_general x128 -> x0, matrix products: 218 us -> none  [the longest x32 133 us: evaluate(): jnp.einsum('qhak,qkhd->qahd', probs, values, preferred_element_type=jnp.f...]
    sub x32 -> x0, matrix products: 169 us -> none  [evaluate(): expo = jnp.exp(scores - top)]
    while x353 -> x0, local copies, waits for them, and re-layouts: 53.8 us -> none
    slice x160 -> x2, local copies, waits for them, and re-layouts: 51.1 us -> 1.37 us  [the longest x1 0.69 us: local(): g[0:4, :, None]]
    all_gather x2 -> x0, blocking collectives: 44.2 us -> none  [the longest x1 24.9 us: local(): lists = lax.all_gather(key_blocks, 'state', axis=0, tiled=True)]
    unnamed x1 -> x0, blocking collectives: 34.1 us -> none
    dynamic_slice x64 -> x0, local copies, waits for them, and re-layouts: 31.6 us -> none  [the longest x32 17.7 us: local(): lax.map(one_config, (feats.reshape(count * walkers, atoms, width), lists....]
  transfers between devices with their start and end apart: 1 -> 0, of which waited for: 1 -> 0; matrix products, arithmetic and copies ran while one was open for 0% -> 0% of each run, Pallas kernels for 0% -> 0%
where the time goes in v1:
time: 275 us
  Pallas kernels  259 us (94%)
  local copies, waits for them, and re-layouts  13.2 us (5%)
    pallas_call x1, Pallas kernels, rest(): pl.pallas_call(functools.partial(rest_kernel, states), out_shape=jax.Shap...  193 us
    pallas_call x1, Pallas kernels, gather(): pl.pallas_call(functools.partial(gather_kernel, states), out_shape=(jax.S...  43.7 us
    pallas_call x1, Pallas kernels, solve(): pl.pallas_call(functools.partial(solve_kernel, states, walks), out_shape=...  21.7 us
    unnamed x16, local copies, waits for them, and re-layouts  9.75 us

profile of v1, /device:TPU:0, one launch (start us, length us, event | category | flops | bytes accessed | tf_op | source)
XLA Modules:
  0.0 274.6 jit_solution(9210491887404929638)
XLA Ops:
  0.6 0.0 copy-start
  0.6 0.0 copy-start.1
  0.7 0.0 copy-start.2
  0.7 0.0 copy-start.3
  0.7 2.3 copy.14
  3.0 0.7 slice.8
  3.7 1.0 broadcast_in_dim.9.refs_4_
  4.7 2.0 copy.17
  6.8 2.1 copy.16
  8.8 0.7 slice.9
  9.5 0.7 fusion.6
  10.2 0.8 broadcast_in_dim.20.refs_5_
  11.0 0.9 copy.15
  11.9 0.1 copy.12
  12.0 0.1 copy.13
  12.1 0.1 concatenate.18
  12.2 0.0 copy-done.3
  12.2 0.1 fusion.5
  12.3 0.7 pad_maximum_fusion.x_ref
  13.0 43.7 %shard_map.113 = (bf16[16,272,512]{2,1,0:T(8,128)(2,1)}, f32[2,4,128]{2,1,0:T(4,128)}, f32[2,8,256]{2,1,0:T(8,128)}) custom-call(bf16[272,512]{1,0:T(8,128)(2,1)} %pad_maximum_fusion.x_ref, bf16[2,768,256]{2,1,0:T(8,128)(2,1)} %bitcast.26, bf16[2,256,256]{2,1,0:T(8,128)(2,1)} %bitcast.32, bf16[2,512,256]{2,1,0:T(8,128)(2,1)} %bitcast.30, ...), custom_call_target="tpu_custom_call" | custom-call | tf_op jit(solution)/shard_map/pallas_call | solution.py:309
  56.8 193.2 %shard_map.114.refs_0_ = f32[2,16,128]{2,1,0:T(8,128)} custom-call(bf16[16,272,512]{2,1,0:T(8,128)(2,1)} %get-tuple-element.7.all_ref, f32[2,4,128]{2,1,0:T(4,128)} %get-tuple-element.8.early, f32[2,8,256]{2,1,0:T(8,128)} %get-tuple-element.9.lims, bf16[2,768,256]{2,1,0:T(8,128)(2,1)} %bitcast.27, bf16[2,256,256]{2,1,0:T(8,128)(2,1)} %bitcast.33, ...), custom_call_target="tpu_custom_call" | custom-call | tf_op jit(solution)/shard_map/pallas_call | solution.py:345
  250.6 21.7 %shard_map.115 = (f32[1,16]{1,0:T(1,128)}, f32[1,16]{1,0:T(1,128)}) custom-call(f32[2,16,128]{2,1,0:T(8,128)} %shard_map.114.refs_0_, f32[1,1]{1,0:T(1,128)S(6)} %copy.23.refs_1_), custom_call_target="tpu_custom_call" | custom-call | tf_op jit(solution)/shard_map/pallas_call | solution.py:428
  272.3 1.1 copy.24
  273.4 1.2 copy.25
  (6 shorter events, 0.0 us)
Async XLA Ops:
  0.6 10.4 %copy-start = (bf16[1,2,256,256]{3,2,1,0:T(8,128)(2,1)S(1)}, bf16[1,2,256,256]{3,2,1,0:T(8,128)(2,1)}, u32[]{:S(2)}) copy-start(bf16[1,2,256,256]{3,2,1,0:T(8,128)(2,1)} %param.15) | copy-start | bytes 786436
  0.6 11.2 %copy-start.1 = (bf16[1,1,512,256]{3,2,1,0:T(8,128)(2,1)S(1)}, bf16[1,1,512,256]{3,2,1,0:T(8,128)(2,1)}, u32[]{:S(2)}) copy-start(bf16[1,1,512,256]{3,2,1,0:T(8,128)(2,1)} %param.10) | copy-start | bytes 786436
  0.7 11.4 %copy-start.2 = (s32[1,1,4,3]{2,1,3,0:T(1,128)S(1)}, s32[1,1,4,3]{2,1,3,0:T(1,128)}, u32[]{:S(2)}) copy-start(s32[1,1,4,3]{2,1,3,0:T(1,128)} %param.11) | copy-start | bytes 148
  0.7 11.6 %copy-start.3 = (s32[1,1,4]{2,1,0:T(1,128)S(1)}, s32[1,1,4]{2,1,0:T(1,128)}, u32[]{:S(2)}) copy-start(s32[1,1,4]{2,1,0:T(1,128)} %param.12) | copy-start | bytes 52

commit v2 on v1

--- a/solution.py
+++ b/solution.py
@@ -1,4 +1,5 @@
 import functools
+import itertools
 
 import jax
 import jax.numpy as jnp
@@ -14,7 +15,12 @@
 H = 8
 SLOTS = 3
 EXTRA = 16
-EARLY = 4
+COUNTS = 8
+EARLY = 6
+AHEAD = 8
+OFFSETS = (0, 1, 4, 5, 12, 13, 2, 3, 6, 7, 14, 15, 8, 9, 10, 11)
+WAVES = ((1, 2, 4, 6), (8, 10, 12), (14,))
+BEFORE = ((), (2,), (4,), (6,), (8,), (10, 12))
 QS = 1.4426950408889634 / 32.0**0.5
 bf = jnp.bfloat16
 f32 = jnp.float32
@@ -39,13 +45,37 @@
 
 class Net:
     def __init__(self, weights, scratch):
-        self.wqkv, self.wo, self.wu, self.wd, self.gn, self.gr = weights
-        self.h, self.k, self.v, self.qx, self.a, self.lim, self.ivm, self.ism, self.isem, self.xbuf, self.xsem = scratch
+        self.raw = weights
+        self.wqkv, self.wo, self.wu, self.wd, self.gn, self.gr = scratch[:6]
+        self.h, self.k, self.v, self.qx, self.a, self.lim = scratch[6:12]
+        self.ivm, self.ism, self.isem, self.xbuf, self.xsem = scratch[12:]
 
     def clear(self):
         self.qx[...] = jnp.zeros(self.qx.shape, bf)
         self.v[...] = jnp.ones(self.v.shape, bf)
         self.lim[...] = jnp.ones(self.lim.shape, f32)
+
+    def prepare(self):
+        *mats, gains, readouts = self.raw
+
+        def layer(l, _):
+            for w, t in zip(mats, (self.wqkv, self.wo, self.wu, self.wd)):
+                for r in range(0, w.shape[1], 256):
+                    for c in range(0, w.shape[2], 256):
+                        tile = w[l, r : r + 256, c : c + 256].T
+                        t[l, c : c + 256, r : r + 256] = tile * bf(0.5) if t is self.wd else tile
+            return 0
+
+        lax.fori_loop(0, 2, layer, 0)
+
+        def column(row):
+            return jnp.broadcast_to(row, (128, D)).T
+
+        for r in range(4):
+            self.gn[r] = column(gains[r : r + 1, :])
+        last = gains[4:5, :] * (1.0 / A**0.5)
+        for t in range(2):
+            self.gr[t] = column(last * readouts[t : t + 1, :])
 
     def ints(self, s):
         self.ivm[...] = self.xbuf[s, D : D + EXTRA, 0:128].astype(f32).astype(jnp.int32)
@@ -84,60 +114,53 @@
     def emit(self, o, b, p):
         den = o[64:72, :]
         inv = 1.0 / den[0:1]
-        lanes = pl.ds(pl.multiple_of(b * 128, 128), 128)
+        lanes = pl.ds(b * 128 if isinstance(b, int) else pl.multiple_of(b * 128, 128), 128)
         self.a[p * 64 : p * 64 + 32, lanes] = (o[0:32, :128] * inv[:, :128]).astype(bf)
         self.a[p * 64 + 32 : p * 64 + 64, lanes] = (o[32:64, 128:] * inv[:, 128:]).astype(bf)
         return den
 
     def attend(self, items, safe):
-        units = [(b, kbs, keep, p) for p in range(4) for b, kbs, keep in items]
-        ss = [self.scores(b, kbs, p) for b, kbs, _, p in units]
-        outs = [self.mix(s, kbs, p, keep, safe) for s, (_, kbs, keep, p) in zip(ss, units)]
-        dens = [self.emit(o, b, p) for o, (b, _, _, p) in zip(outs, units)]
+        units = [(b, kbs, keep, p) for b, kbs, keep in items for p in range(4)]
+        ss = [self.scores(b, kbs, p) for b, kbs, _, p in units[:AHEAD]]
+        dens = []
+        for n, (b, kbs, keep, p) in enumerate(units):
+            if n + AHEAD < len(units):
+                later = units[n + AHEAD]
+                ss.append(self.scores(later[0], later[1], later[3]))
+            dens.append(self.emit(self.mix(ss[n], kbs, p, keep, safe), b, p))
         if not safe:
             self.lim[0] = jnp.minimum(self.lim[0], functools.reduce(jnp.minimum, dens))
             self.lim[1] = jnp.maximum(self.lim[1], functools.reduce(jnp.maximum, dens))
 
     def attention_masked(self, s):
-        def two(g, _):
-            items = []
-            for b in (2 * g, 2 * g + 1):
-                count = self.ism[s, 0, SLOTS * NB + b]
-                kbs = [jnp.clip(self.ism[s, 0, b * SLOTS + t], 0, NB - 1) for t in range(SLOTS)]
-                items.append((b, kbs, [count > t for t in range(SLOTS)]))
-            self.attend(items, False)
-            return 0
-
-        lax.fori_loop(0, NB // 2, two, 0)
+        items = []
+        for b in range(NB):
+            count = self.ism[s, COUNTS, b]
+            kbs = [jnp.clip(self.ism[s, b, t], 0, NB - 1) for t in range(SLOTS)]
+            items.append((b, kbs, [count > t for t in range(SLOTS)]))
+        self.attend(items, False)
 
     def attention(self, s, safe):
-        def two(g, _):
-            x, y = self.ism[s, 0, SLOTS * NB + 2 * g], self.ism[s, 0, SLOTS * NB + 2 * g + 1]
-            swap = (y > x).astype(jnp.int32)
-            more, less = 2 * g + swap, 2 * g + 1 - swap
-            most, least = jnp.maximum(x, y), jnp.minimum(x, y)
-
-            def run(c0, c1):
-                lists = [(b, [self.ism[s, 0, b * SLOTS + t] for t in range(c)], None) for b, c in ((more, c0), (less, c1))]
-                self.attend(lists, safe)
-
-            for c0 in range(1, SLOTS + 1):
-                for c1 in range(1, c0 + 1):
-                    pl.when((most == c0) & (least == c1))(functools.partial(run, c0, c1))
-            return 0
-
-        lax.fori_loop(0, NB // 2, two, 0)
+        count = [self.ism[s, COUNTS, b] for b in range(1, NB)]
+        block = [jnp.int32(b) for b in range(1, NB)]
+        for x, y in ((0, 1), (1, 2), (0, 1)):
+            swap = count[y] > count[x]
+            for seq in (count, block):
+                seq[x], seq[y] = jnp.where(swap, seq[y], seq[x]), jnp.where(swap, seq[x], seq[y])
+        for case in itertools.combinations_with_replacement(range(SLOTS, 0, -1), NB - 1):
+
+            @pl.when((count[0] == case[0]) & (count[1] == case[1]) & (count[2] == case[2]))
+            def _(case=case):
+                todo = zip([0, *block], (SLOTS, *case))
+                self.attend([(b, [self.ism[s, b, t] for t in range(c)], None) for b, c in todo], safe)
 
     def feed(self, l, then):
-        cols = [slice(c * 256, c * 256 + 256) for c in range(2)]
-        hs = [self.h[:, s] + mm(self.wo[l], self.a[:, s]) for s in cols]
-        us = [mm(self.wu[l], norm(h, self.gn[2 * l + 1])) for h in hs]
+        h = self.h[...] + mm(self.wo[l], self.a[...])
+        u = mm(self.wu[l], norm(h, self.gn[2 * l + 1]))
+        z = u * (0.7978845608028654 + 0.035677408136300125 * (u * u))
+        h = h + mm(self.wd[l], (u + u * jnp.tanh(z)).astype(bf))
         for c in range(2):
-            u = us[c]
-            z = u * (0.7978845608028654 + 0.035677408136300125 * (u * u))
-            half = 0.5 * u
-            g = (half + half * jnp.tanh(z)).astype(bf)
-            then(c, hs[c] + mm(self.wd[l], g))
+            then(c, h[:, c * 256 : c * 256 + 256])
 
     def final(self, h, sums):
         r = rscale(h)
@@ -177,6 +200,11 @@
 
                 @pl.when(l == 0)
                 def _():
+                    @pl.when(i + 1 < first + count)
+                    def _():
+                        fetch(i + 1).wait()
+                        self.ints(1 - s).start()
+
                     def then(c, h):
                         self.h[:, c * 256 : c * 256 + 256] = h
                         self.project(1, c, h)
@@ -185,13 +213,6 @@
 
                 @pl.when(l == 1)
                 def _():
-                    @pl.when(i + 1 < first + count)
-                    def _():
-                        fetch(i + 1).wait()
-                        lists = self.ints(1 - s)
-                        lists.start()
-                        lists.wait()
-
                     sums = [[0.0, 0.0]]
                     later = begin(1 - s)
                     for c in range(2):
@@ -202,6 +223,10 @@
                     for t in range(2):
                         out[t, pl.ds(i - at, 1)] = sums[-1][t]
 
+                    @pl.when(i + 1 < first + count)
+                    def _():
+                        pltpu.make_async_copy(self.ivm, self.ism.at[1 - s], self.isem).wait()
+
                 return 0
 
             lax.fori_loop(0, 2, layer, 0)
@@ -212,6 +237,12 @@
 
 def scratch():
     return [
+        pltpu.VMEM((2, 3 * D, D), bf),
+        pltpu.VMEM((2, D, D), bf),
+        pltpu.VMEM((2, 2 * D, D), bf),
+        pltpu.VMEM((2, D, 2 * D), bf),
+        pltpu.VMEM((4, D, 128), f32),
+        pltpu.VMEM((2, D, 128), f32),
         pltpu.VMEM((D, A), f32),
         pltpu.VMEM((NB, B, D), bf),
         pltpu.VMEM((NB, 4, 80, B), bf),
@@ -234,24 +265,29 @@
     return out
 
 
-def gather_kernel(states, x_ref, *refs):
+def gather_kernel(states, feats, lists, counts, *refs):
     weights, (all_ref, out, lims) = refs[:6], refs[6:9]
-    net = Net(weights, refs[9:20])
-    ssem, rsem, csem = refs[20:]
+    net = Net(weights, refs[9:26])
+    x_ref, ssem, rsem, csem = refs[26:]
     me, mw = lax.axis_index("state"), lax.axis_index("walk")
     barrier = pltpu.get_barrier_semaphore()
     partners = [1] + list(range(2, states, 2))
     for k in partners:
-        pl.semaphore_signal(barrier, inc=1, device_id=(flip(me, k), mw), device_id_type=MESH)
+        pl.semaphore_signal(barrier, inc=1, device_id=(flip(me, OFFSETS[k]), mw), device_id_type=MESH)
+    x_ref[0:D, :] = feats[...].T
+    net.ivm[...] = jnp.zeros(net.ivm.shape, jnp.int32)
+    net.ivm[0:NB, 0:SLOTS] = lists[...]
+    net.ivm[COUNTS : COUNTS + 1, 0:NB] = counts[...]
+    x_ref[D : D + EXTRA, :] = jnp.zeros((EXTRA, A), bf)
+    x_ref[D : D + EXTRA, 0:128] = net.ivm[...].astype(f32).astype(bf)
     own = pltpu.make_async_copy(x_ref, all_ref.at[0], csem)
     own.start()
-    net.clear()
     pl.semaphore_wait(barrier, len(partners))
 
     def send(k):
         return pltpu.make_async_remote_copy(
             src_ref=x_ref, dst_ref=all_ref.at[k], send_sem=ssem.at[k], recv_sem=rsem.at[k],
-            device_id=(flip(me, k), mw), device_id_type=MESH,
+            device_id=(flip(me, OFFSETS[k]), mw), device_id_type=MESH,
         )
 
     def relay(k):
@@ -260,9 +296,15 @@
             device_id=(flip(me, 1), mw), device_id_type=MESH,
         )
 
-    order = [1] + [k for k in ORDER if k < states]
-    for k in order:
+    def landed(k):
+        send(k).wait_recv()
+        if k > 1:
+            relay(k).start()
+
+    for k in WAVES[0]:
         send(k).start()
+    net.clear()
+    net.prepare()
     own.wait()
 
     def fetch(i):
@@ -271,41 +313,33 @@
 
     def between(i):
         for n in range(EARLY):
+
             @pl.when(i == n)
-            def _():
-                if n + 1 < EARLY:
-                    if n == 0:
-                        send(1).wait_recv()
-                    if n == 1:
-                        send(2).wait_recv()
-                        relay(2).start()
-                    if n == 2:
-                        relay(2).wait_recv()
+            def _(n=n):
+                for k in WAVES[n + 1] if n + 1 < len(WAVES) else ():
+                    send(k).start()
+                if n == 0:
+                    landed(1)
                 for k in BEFORE[n]:
-                    send(k).wait_recv()
-                    relay(k).start()
+                    landed(k)
+                if n % 2 == 0 and 0 < n < EARLY - 1:
+                    relay(n).wait_recv()
 
     net.run(0, EARLY, net.attention_masked, fetch, out, 0, between)
-    done = {2} | {k for ks in BEFORE for k in ks}
-    for k in order[1:]:
-        if k not in done:
-            send(k).wait_recv()
-            relay(k).start()
-    for k in order[1:]:
-        if k != 2:
+    for k in partners[1:]:
+        if all(k not in ks for ks in BEFORE):
+            landed(k)
+    for k in partners[1:]:
+        if k + 1 >= EARLY:
             relay(k).wait_recv()
-    for k in order:
+    for k in partners:
         send(k).wait_send()
-    for k in order[1:]:
+    for k in partners[1:]:
         relay(k).wait_send()
     lims[...] = net.lim[...]
 
 
-ORDER = (2, 4, 12, 6, 14, 8, 10)
-BEFORE = ((), (), (4, 12), (6, 14))
-
-
-def gather(x, ws, states):
+def gather(feats, lists, counts, ws, states):
     return pl.pallas_call(
         functools.partial(gather_kernel, states),
         out_shape=(
@@ -313,18 +347,20 @@
             jax.ShapeDtypeStruct((2, EARLY, 128), f32),
             jax.ShapeDtypeStruct((2, 8, 2 * B), f32),
         ),
-        in_specs=[ANY] + [V] * 6,
+        in_specs=[V] * 9,
         out_specs=(ANY, V, V),
         scratch_shapes=scratch()
+        + [pltpu.VMEM((D + EXTRA, A), bf)]
         + [pltpu.SemaphoreType.DMA((states,)), pltpu.SemaphoreType.DMA((states,)), pltpu.SemaphoreType.DMA],
         compiler_params=pltpu.CompilerParams(collective_id=1, has_side_effects=True, vmem_limit_bytes=56 * 2**20),
-    )(x, *ws)
+    )(feats, lists, counts, *ws)
 
 
 def rest_kernel(states, all_ref, early, lims, *refs):
     weights, out = refs[:6], refs[6]
     net = Net(weights, refs[7:])
     net.clear()
+    net.prepare()
 
     def fetch(i):
         s = lax.rem(i, 2)
@@ -363,7 +399,8 @@
 
     lane = lax.broadcasted_iota(jnp.int32, (states, 128), 1)
     row_at = lax.broadcasted_iota(jnp.int32, (states, 128), 0)
-    config = jnp.bitwise_xor(row_at, me)
+    offset = functools.reduce(lambda a, p: jnp.where(row_at == p, OFFSETS[p], a), range(states), row_at)
+    config = jnp.bitwise_xor(offset, me)
 
     def spread(t):
         value = jnp.sum(parts[t], axis=1, keepdims=True)
@@ -441,19 +478,8 @@
 
 def local(features, key_blocks, block_counts, potential, w_qkv, w_out, w_up, w_down, gains, readouts):
     states, walks = lax.axis_size("state"), lax.axis_size("walk")
-    ints = jnp.concatenate([key_blocks.reshape(-1), block_counts.reshape(-1)]).astype(bf)
-    extra = jnp.pad(ints[None], ((0, EXTRA - 1), (0, A - ints.shape[0])))
-    mine = jnp.concatenate([features[0, 0].T, extra], axis=0)
-    g = gains[0]
-    ws = (
-        w_qkv[0].swapaxes(1, 2),
-        w_out[0].swapaxes(1, 2),
-        w_up[0].swapaxes(1, 2),
-        w_down[0].swapaxes(1, 2),
-        jnp.broadcast_to(g[0:4, :, None], (4, D, 128)),
-        jnp.broadcast_to((g[4] * readouts[0] / jnp.sqrt(f32(A)))[:, :, None], (2, D, 128)),
-    )
-    every, early, lims = gather(mine, ws, states)
+    ws = (w_qkv[0], w_out[0], w_up[0], w_down[0], gains[0], readouts[0])
+    every, early, lims = gather(features[0, 0], key_blocks[0, 0], block_counts[0], ws, states)
     parts = rest(every, early, lims, ws, states)
     energy, mean = solve(parts, potential, states, walks)
     return energy[:, :, None], mean

time: 275 us -> 223 us (0.81)
  Pallas kernels: 259 us -> 216 us
  local copies, waits for them, and re-layouts: 13.2 us -> 4.93 us
    pallas_call x1, Pallas kernels: 193 us -> 146 us  [rest(): pl.pallas_call(functools.partial(rest_kernel, states), out_shape=jax.Shap...]
    pallas_call x1, Pallas kernels: 43.7 us -> 52 us  [gather(): pl.pallas_call(functools.partial(gather_kernel, states), out_shape=(jax.S...]
    unnamed x16 -> x4, local copies, waits for them, and re-layouts: 9.75 us -> 4.93 us
    pallas_call x1, Pallas kernels: 21.7 us -> 18.3 us  [solve(): pl.pallas_call(functools.partial(solve_kernel, states, walks), out_shape=...]
where the time goes in v2:
time: 223 us; the launch traced here: 222 us
  Pallas kernels  216 us (97%)
  local copies, waits for them, and re-layouts  4.93 us (2%)
    pallas_call x1, Pallas kernels, rest(): pl.pallas_call(functools.partial(rest_kernel, states), out_shape=jax.Shap...  146 us
    pallas_call x1, Pallas kernels, gather(): pl.pallas_call(functools.partial(gather_kernel, states), out_shape=(jax.S...  52 us
    pallas_call x1, Pallas kernels, solve(): pl.pallas_call(functools.partial(solve_kernel, states, walks), out_shape=...  18.3 us
    unnamed x4, local copies, waits for them, and re-layouts  4.93 us

profile of v2, /device:TPU:0, one launch (start us, length us, event | category | flops | bytes accessed | tf_op | source)
XLA Modules:
  0.0 222.4 jit_solution(15064099425572088898)
XLA Ops:
  0.6 1.3 copy.15
  1.9 1.3 copy.12
  3.2 52.0 %shard_map.113 = (bf16[16,272,512]{2,1,0:T(8,128)(2,1)}, f32[2,6,128]{2,1,0:T(8,128)}, f32[2,8,256]{2,1,0:T(8,128)}) custom-call(bf16[512,256]{1,0:T(8,128)(2,1)} %bitcast.20, s32[4,3]{1,0:T(4,128)} %bitcast.25, s32[1,4]{1,0:T(1,128)} %bitcast.26, bf16[2,256,768]{2,1,0:T(8,128)(2,1)} %bitcast.12, bf16[2,256,256]{2,1,0:T(8,128)(2,1)} %bitcast.18, ...), custom_call_target="tpu_custom_call" | custom-call | tf_op jit(solution)/shard_map/pallas_call | solution.py:343
  55.2 145.9 %shard_map.114.refs_0_ = f32[2,16,128]{2,1,0:T(8,128)} custom-call(bf16[16,272,512]{2,1,0:T(8,128)(2,1)} %get-tuple-element.7.all_ref, f32[2,6,128]{2,1,0:T(8,128)} %get-tuple-element.8.early, f32[2,8,256]{2,1,0:T(8,128)} %get-tuple-element.9.lims, bf16[2,256,768]{2,1,0:T(8,128)(2,1)} %bitcast.13, bf16[2,256,256]{2,1,0:T(8,128)(2,1)} %bitcast.19, ...), custom_call_target="tpu_custom_call" | custom-call | tf_op jit(solution)/shard_map/pallas_call | solution.py:381
  201.8 18.3 %shard_map.115 = (f32[1,16]{1,0:T(1,128)}, f32[1,16]{1,0:T(1,128)}) custom-call(f32[2,16,128]{2,1,0:T(8,128)} %shard_map.114.refs_0_, f32[1,1]{1,0:T(1,128)S(6)} %copy.18.refs_1_), custom_call_target="tpu_custom_call" | custom-call | tf_op jit(solution)/shard_map/pallas_call | solution.py:465
  220.1 1.1 copy.19
  221.2 1.2 copy.20

commit v3 on v2

--- a/solution.py
+++ b/solution.py
@@ -16,11 +16,10 @@
 SLOTS = 3
 EXTRA = 16
 COUNTS = 8
-EARLY = 6
+EARLY = 5
 AHEAD = 8
 OFFSETS = (0, 1, 4, 5, 12, 13, 2, 3, 6, 7, 14, 15, 8, 9, 10, 11)
-WAVES = ((1, 2, 4, 6), (8, 10, 12), (14,))
-BEFORE = ((), (2,), (4,), (6,), (8,), (10, 12))
+DIRECT = (1, 2, 4, 6)
 QS = 1.4426950408889634 / 32.0**0.5
 bf = jnp.bfloat16
 f32 = jnp.float32
@@ -72,8 +71,8 @@
             return jnp.broadcast_to(row, (128, D)).T
 
         for r in range(4):
-            self.gn[r] = column(gains[r : r + 1, :])
-        last = gains[4:5, :] * (1.0 / A**0.5)
+            self.gn[r] = column(gains[r])
+        last = gains[4] * (1.0 / A**0.5)
         for t in range(2):
             self.gr[t] = column(last * readouts[t : t + 1, :])
 
@@ -136,7 +135,7 @@
         items = []
         for b in range(NB):
             count = self.ism[s, COUNTS, b]
-            kbs = [jnp.clip(self.ism[s, b, t], 0, NB - 1) for t in range(SLOTS)]
+            kbs = [jnp.clip(self.ism[s, t, b], 0, NB - 1) for t in range(SLOTS)]
             items.append((b, kbs, [count > t for t in range(SLOTS)]))
         self.attend(items, False)
 
@@ -152,7 +151,7 @@
             @pl.when((count[0] == case[0]) & (count[1] == case[1]) & (count[2] == case[2]))
             def _(case=case):
                 todo = zip([0, *block], (SLOTS, *case))
-                self.attend([(b, [self.ism[s, b, t] for t in range(c)], None) for b, c in todo], safe)
+                self.attend([(b, [self.ism[s, t, b] for t in range(c)], None) for b, c in todo], safe)
 
     def feed(self, l, then):
         h = self.h[...] + mm(self.wo[l], self.a[...])
@@ -271,38 +270,46 @@
     x_ref, ssem, rsem, csem = refs[26:]
     me, mw = lax.axis_index("state"), lax.axis_index("walk")
     barrier = pltpu.get_barrier_semaphore()
-    partners = [1] + list(range(2, states, 2))
-    for k in partners:
+    for k in DIRECT:
         pl.semaphore_signal(barrier, inc=1, device_id=(flip(me, OFFSETS[k]), mw), device_id_type=MESH)
     x_ref[0:D, :] = feats[...].T
     net.ivm[...] = jnp.zeros(net.ivm.shape, jnp.int32)
-    net.ivm[0:NB, 0:SLOTS] = lists[...]
+    for t in range(SLOTS):
+        net.ivm[t : t + 1, 0:NB] = lists[t]
     net.ivm[COUNTS : COUNTS + 1, 0:NB] = counts[...]
     x_ref[D : D + EXTRA, :] = jnp.zeros((EXTRA, A), bf)
     x_ref[D : D + EXTRA, 0:128] = net.ivm[...].astype(f32).astype(bf)
     own = pltpu.make_async_copy(x_ref, all_ref.at[0], csem)
     own.start()
-    pl.semaphore_wait(barrier, len(partners))
-
-    def send(k):
+    pl.semaphore_wait(barrier, len(DIRECT))
+
+    near = lax.rem(lax.rem(lax.div(me, 4), 2) + lax.rem(me, 2), 2) == 0
+    onward = jnp.where(near, flip(me, 4), flip(me, 12))
+
+    def push(src, k, device):
         return pltpu.make_async_remote_copy(
-            src_ref=x_ref, dst_ref=all_ref.at[k], send_sem=ssem.at[k], recv_sem=rsem.at[k],
-            device_id=(flip(me, OFFSETS[k]), mw), device_id_type=MESH,
+            src_ref=src, dst_ref=all_ref.at[k], send_sem=ssem.at[k], recv_sem=rsem.at[k],
+            device_id=(device, mw), device_id_type=MESH,
         )
 
-    def relay(k):
-        return pltpu.make_async_remote_copy(
-            src_ref=all_ref.at[k], dst_ref=all_ref.at[k + 1], send_sem=ssem.at[k + 1], recv_sem=rsem.at[k + 1],
-            device_id=(flip(me, 1), mw), device_id_type=MESH,
-        )
-
-    def landed(k):
-        send(k).wait_recv()
-        if k > 1:
-            relay(k).start()
-
-    for k in WAVES[0]:
-        send(k).start()
+    def copy(k):
+        if k in DIRECT:
+            return push(x_ref, k, flip(me, OFFSETS[k]))
+        if k % 2:
+            return push(all_ref.at[k - 1], k, flip(me, 1))
+        if k in (8, 10):
+            return push(all_ref.at[6], k, flip(me, 4 if k == 8 else 12))
+        one, other = (2, 4) if k == 12 else (8, 10)
+        return push(all_ref.at[jnp.where(near, other, one)], k, onward)
+
+    def landed(*slots):
+        for k in slots:
+            copy(k).wait_recv()
+            if k % 2 == 0:
+                copy(k + 1).start()
+
+    for k in DIRECT:
+        copy(k).start()
     net.clear()
     net.prepare()
     own.wait()
@@ -312,30 +319,37 @@
         return pltpu.make_async_copy(all_ref.at[i], net.xbuf.at[s], net.xsem.at[s])
 
     def between(i):
-        for n in range(EARLY):
-
-            @pl.when(i == n)
-            def _(n=n):
-                for k in WAVES[n + 1] if n + 1 < len(WAVES) else ():
-                    send(k).start()
-                if n == 0:
-                    landed(1)
-                for k in BEFORE[n]:
-                    landed(k)
-                if n % 2 == 0 and 0 < n < EARLY - 1:
-                    relay(n).wait_recv()
+        @pl.when(i == 0)
+        def _():
+            landed(1)
+
+        @pl.when(i == 1)
+        def _():
+            landed(2, 4)
+            copy(12).start()
+
+        @pl.when(i == 2)
+        def _():
+            landed(6)
+            copy(8).start()
+            copy(10).start()
+            copy(3).wait_recv()
+
+        @pl.when(i == 3)
+        def _():
+            landed(8, 10)
+            copy(14).start()
+            landed(12)
+
+        @pl.when(i == 4)
+        def _():
+            landed(14)
 
     net.run(0, EARLY, net.attention_masked, fetch, out, 0, between)
-    for k in partners[1:]:
-        if all(k not in ks for ks in BEFORE):
-            landed(k)
-    for k in partners[1:]:
-        if k + 1 >= EARLY:
-            relay(k).wait_recv()
-    for k in partners:
-        send(k).wait_send()
-    for k in partners[1:]:
-        relay(k).wait_send()
+    for k in range(5, states, 2):
+        copy(k).wait_recv()
+    for k in range(1, states):
+        copy(k).wait_send()
     lims[...] = net.lim[...]
 
 
@@ -436,7 +450,7 @@
         m = jnp.where(row_at == k, scaled, m - column * scaled)
     mine = jnp.sum(jnp.where(row_at == me, m, 0.0), axis=0, keepdims=True)
     mine = jnp.where(lane1 == me, mine + pot[...], mine)
-    energy[...] = mine[:, :states]
+    energy[...] = mine
     rows[pl.ds(mw, 1), :] = mine
 
     def send_row(d):
@@ -453,7 +467,7 @@
             src_ref=rows.at[pl.ds(mw, 1)], dst_ref=rows.at[pl.ds(came, 1)], send_sem=wssem.at[d], recv_sem=wrsem.at[d],
             device_id=(me, lax.rem(mw + d, walks)), device_id_type=MESH,
         ).wait_recv()
-    mean[...] = (jnp.sum(rows[...], axis=0, keepdims=True) * (1.0 / walks))[:, :states]
+    mean[...] = jnp.sum(rows[...], axis=0, keepdims=True) * (1.0 / walks)
     for d in range(1, states):
         send(d).wait_send()
     for d in range(1, walks):
@@ -464,7 +478,7 @@
     dma = pltpu.SemaphoreType.DMA
     return pl.pallas_call(
         functools.partial(solve_kernel, states, walks),
-        out_shape=(jax.ShapeDtypeStruct((1, states), f32), jax.ShapeDtypeStruct((1, states), f32)),
+        out_shape=(jax.ShapeDtypeStruct((1, 128), f32), jax.ShapeDtypeStruct((1, 128), f32)),
         in_specs=[V, V],
         out_specs=(V, V),
         scratch_shapes=[
@@ -476,12 +490,23 @@
     )(parts, potential)
 
 
+def trim_kernel(energy, mean, energy_out, mean_out):
+    n = energy_out.shape[1]
+    energy_out[...] = energy[:, :n]
+    mean_out[...] = mean[:, :n]
+
+
+def trim(energy, mean, states):
+    shape = jax.ShapeDtypeStruct((1, states), f32)
+    return pl.pallas_call(trim_kernel, out_shape=(shape, shape), in_specs=[V, V], out_specs=(V, V))(energy, mean)
+
+
 def local(features, key_blocks, block_counts, potential, w_qkv, w_out, w_up, w_down, gains, readouts):
     states, walks = lax.axis_size("state"), lax.axis_size("walk")
-    ws = (w_qkv[0], w_out[0], w_up[0], w_down[0], gains[0], readouts[0])
-    every, early, lims = gather(features[0, 0], key_blocks[0, 0], block_counts[0], ws, states)
+    ws = (w_qkv[0], w_out[0], w_up[0], w_down[0], gains.transpose(1, 0, 2), readouts[0])
+    every, early, lims = gather(features[0, 0], key_blocks[0].transpose(2, 0, 1), block_counts[0], ws, states)
     parts = rest(every, early, lims, ws, states)
-    energy, mean = solve(parts, potential, states, walks)
+    energy, mean = trim(*solve(parts, potential, states, walks), states)
     return energy[:, :, None], mean
 
 

time: 223 us -> 214 us (0.960)
  local copies, waits for them, and re-layouts: 4.93 us -> 0 us
  Pallas kernels: 216 us -> 212 us
    pallas_call x1, Pallas kernels: 52 us -> 41 us  [gather(): pl.pallas_call(functools.partial(gather_kernel, states), out_shape=(jax.S...]
    pallas_call x1, Pallas kernels: 146 us -> 156 us  [rest(): pl.pallas_call(functools.partial(rest_kernel, states), out_shape=jax.Shap...]
    unnamed x4 -> x0, local copies, waits for them, and re-layouts: 4.93 us -> none
    pallas_call x1, Pallas kernels: 18.3 us -> 14.1 us  [solve(): pl.pallas_call(functools.partial(solve_kernel, states, walks), out_shape=...]
where the time goes in v3:
time: 214 us; the launch traced here: 213 us
  Pallas kernels  212 us (99%)
    pallas_call x1, Pallas kernels, rest(): pl.pallas_call(functools.partial(rest_kernel, states), out_shape=jax.Shap...  156 us
    pallas_call x1, Pallas kernels, gather(): pl.pallas_call(functools.partial(gather_kernel, states), out_shape=(jax.S...  41 us
    pallas_call x1, Pallas kernels, solve(): pl.pallas_call(functools.partial(solve_kernel, states, walks), out_shape=...  14.1 us

profile of v3, /device:TPU:0, one launch (start us, length us, event | category | flops | bytes accessed | tf_op | source)
XLA Modules:
  0.0 213.5 jit_solution(4781339767761247415)
XLA Ops:
  0.6 41.0 %shard_map.113 = (bf16[16,272,512]{2,1,0:T(8,128)(2,1)}, f32[2,5,128]{2,1,0:T(8,128)}, f32[2,8,256]{2,1,0:T(8,128)}) custom-call(bf16[512,256]{1,0:T(8,128)(2,1)} %bitcast.20, s32[3,1,4]{2,1,0:T(1,128)} %bitcast.25, s32[1,4]{1,0:T(1,128)} %bitcast.26, bf16[2,256,768]{2,1,0:T(8,128)(2,1)} %bitcast.12, bf16[2,256,256]{2,1,0:T(8,128)(2,1)} %bitcast.18, ...), custom_call_target="tpu_custom_call" | custom-call | tf_op jit(solution)/shard_map/pallas_call | solution.py:357
  41.6 155.9 %shard_map.114.refs_0_ = f32[2,16,128]{2,1,0:T(8,128)} custom-call(bf16[16,272,512]{2,1,0:T(8,128)(2,1)} %get-tuple-element.9.all_ref, f32[2,5,128]{2,1,0:T(8,128)} %get-tuple-element.10.early, f32[2,8,256]{2,1,0:T(8,128)} %get-tuple-element.11.lims, bf16[2,256,768]{2,1,0:T(8,128)(2,1)} %bitcast.13, bf16[2,256,256]{2,1,0:T(8,128)(2,1)} %bitcast.19, ...), custom_call_target="tpu_custom_call" | custom-call | tf_op jit(solution)/shard_map/pallas_call | solution.py:395
  198.2 14.1 %shard_map.115 = (f32[1,128]{1,0:T(1,128)}, f32[1,128]{1,0:T(1,128)}) custom-call(f32[2,16,128]{2,1,0:T(8,128)} %shard_map.114.refs_0_, f32[1,1]{1,0:T(1,128)S(6)} %copy.12.refs_1_), custom_call_target="tpu_custom_call" | custom-call | tf_op jit(solution)/shard_map/pallas_call | solution.py:479
  212.3 1.2 shard_map.116

commit v4 on v3

--- a/solution.py
+++ b/solution.py
@@ -82,8 +82,8 @@
 
     def project(self, l, c, h):
         n = norm(h, self.gn[2 * l])
+        k = mm(self.wqkv[l, 256:512, :], n).astype(bf).T
         q = (mm(self.wqkv[l, 0:256, :], n) * QS).astype(bf)
-        k = mm(self.wqkv[l, 256:512, :], n).astype(bf).T
         v = mm(self.wqkv[l, 512:768, :], n).astype(bf)
         for head in range(H):
             row, lane = (head % 4) * 32, (head % 2) * 128
@@ -153,9 +153,11 @@
                 todo = zip([0, *block], (SLOTS, *case))
                 self.attend([(b, [self.ism[s, t, b] for t in range(c)], None) for b, c in todo], safe)
 
-    def feed(self, l, then):
+    def feed(self, l, then, fill=(lambda: None, lambda: None)):
         h = self.h[...] + mm(self.wo[l], self.a[...])
+        fill[0]()
         u = mm(self.wu[l], norm(h, self.gn[2 * l + 1]))
+        fill[1]()
         z = u * (0.7978845608028654 + 0.035677408136300125 * (u * u))
         h = h + mm(self.wd[l], (u + u * jnp.tanh(z)).astype(bf))
         for c in range(2):
@@ -214,9 +216,10 @@
                 def _():
                     sums = [[0.0, 0.0]]
                     later = begin(1 - s)
-                    for c in range(2):
-                        self.project(0, c, later[c])
-                    self.feed(1, lambda c, h: sums.append(self.final(h, sums[-1])))
+                    done = []
+                    self.feed(1, lambda c, h: done.append(h), [functools.partial(self.project, 0, c, later[c]) for c in range(2)])
+                    for h in done:
+                        sums.append(self.final(h, sums[-1]))
                     for c in range(2):
                         self.h[:, c * 256 : c * 256 + 256] = later[c]
                     for t in range(2):

time: 214 us -> 205 us (0.958)
  Pallas kernels: 212 us -> 202 us
    pallas_call x1, Pallas kernels: 156 us -> 137 us  [rest(): pl.pallas_call(functools.partial(rest_kernel, states), out_shape=jax.Shap...]
    pallas_call x1, Pallas kernels: 14.1 us -> 24.1 us  [solve(): pl.pallas_call(functools.partial(solve_kernel, states, walks), out_shape=...]
where the time goes in v4:
time: 205 us; the launch traced here: 204 us
  Pallas kernels  202 us (99%)
    pallas_call x1, Pallas kernels, rest(): pl.pallas_call(functools.partial(rest_kernel, states), out_shape=jax.Shap...  137 us
    pallas_call x1, Pallas kernels, gather(): pl.pallas_call(functools.partial(gather_kernel, states), out_shape=(jax.S...  39.9 us
    pallas_call x1, Pallas kernels, solve(): pl.pallas_call(functools.partial(solve_kernel, states, walks), out_shape=...  24.1 us

profile of v4, /device:TPU:0, one launch (start us, length us, event | category | flops | bytes accessed | tf_op | source)
XLA Modules:
  0.0 203.6 jit_solution(17278594490876410077)
XLA Ops:
  0.6 39.9 %shard_map.113 = (bf16[16,272,512]{2,1,0:T(8,128)(2,1)}, f32[2,5,128]{2,1,0:T(8,128)}, f32[2,8,256]{2,1,0:T(8,128)}) custom-call(bf16[512,256]{1,0:T(8,128)(2,1)} %bitcast.20, s32[3,1,4]{2,1,0:T(1,128)} %bitcast.25, s32[1,4]{1,0:T(1,128)} %bitcast.26, bf16[2,256,768]{2,1,0:T(8,128)(2,1)} %bitcast.12, bf16[2,256,256]{2,1,0:T(8,128)(2,1)} %bitcast.18, ...), custom_call_target="tpu_custom_call" | custom-call | tf_op jit(solution)/shard_map/pallas_call | solution.py:360
  40.5 137.1 %shard_map.114.refs_0_ = f32[2,16,128]{2,1,0:T(8,128)} custom-call(bf16[16,272,512]{2,1,0:T(8,128)(2,1)} %get-tuple-element.9.all_ref, f32[2,5,128]{2,1,0:T(8,128)} %get-tuple-element.10.early, f32[2,8,256]{2,1,0:T(8,128)} %get-tuple-element.11.lims, bf16[2,256,768]{2,1,0:T(8,128)(2,1)} %bitcast.13, bf16[2,256,256]{2,1,0:T(8,128)(2,1)} %bitcast.19, ...), custom_call_target="tpu_custom_call" | custom-call | tf_op jit(solution)/shard_map/pallas_call | solution.py:398
  178.3 24.1 %shard_map.115 = (f32[1,128]{1,0:T(1,128)}, f32[1,128]{1,0:T(1,128)}) custom-call(f32[2,16,128]{2,1,0:T(8,128)} %shard_map.114.refs_0_, f32[1,1]{1,0:T(1,128)S(6)} %copy.12.refs_1_), custom_call_target="tpu_custom_call" | custom-call | tf_op jit(solution)/shard_map/pallas_call | solution.py:482
  202.4 1.2 shard_map.116
